TPU v7x, 128 devices: a whole 4x4x4 slice. The times are simulated.
128 devices in a mesh: item: 16 (over z, y), code: 8 (over x, core).
Axes of the slice: x: 4, y: 4, z: 4, core: 2. Of those that a mesh axis runs over, the one named last changes fastest.
Arguments:
- residuals: float32 [256, 65536], P('code', 'item'), may hold values from -6 to 6
- codebook: float32 [256, 65536], P('item', 'code'), may hold values from -6 to 6
- item_weight: float32 [65536], P('item'), may hold values from 1 to 100
- code_capacity: float32 [65536], P('code'), may hold values from 0.25 to 4
- pairs: int32 [1024, 128], P('item', 'code'), may hold values from -1 to 127, as said below
Outputs:
- item_potential: float32 [65536], P('item')
- code_potential: float32 [65536], P('code')
Inputs may be any that keep to these rules, and one draw needn't show every extreme that they name: `pairs`: each entry is -1 (no candidate) or a code block's number within the code shard of its slot column. Within one item block and one code shard the live entries are distinct, the first slot is always live, and between 1 and 8 are live; some device holds exactly 8 live slots in every item block. Every code block is named by some item block.
All inputs are finite; a program needn't handle non-finite values.
Results may differ from a plain program's by a relative error of at most 0.0003.
Values sent between devices are 32-bit elements; how exact they have to be, the bound alone decides.
A program may use at most 128 MiB of HBM per device.

v0:
```python
import math
import jax
import jax.numpy as jnp
from jax import lax
from jax.sharding import PartitionSpec as P

BLOCK = 64
ITERS = 3
masked_score = -1e30
softness_factor = 0.1


def body(residuals, codebook, item_weight, code_capacity, pairs):
    item_columns = lax.all_gather(residuals, "code", axis=0, tiled=True)
    code_cols = lax.all_gather(codebook, "item", axis=0, tiled=True)
    embedding_width = item_columns.shape[0]
    item_count = item_columns.shape[1]
    code_count = code_cols.shape[1]
    item_blocks = item_count // BLOCK
    code_blocks = code_count // BLOCK
    logit_scale = 1.0 / (softness_factor * math.sqrt(embedding_width))
    weight_sum = lax.psum(jnp.sum(item_weight), "item")
    capacity_sum = lax.psum(jnp.sum(code_capacity), "code")
    item_logmass = jnp.log(item_weight) - jnp.log(weight_sum)
    code_logmass = jnp.log(code_capacity) - jnp.log(capacity_sum)
    is_live = pairs >= 0
    safe_ids = jnp.where(is_live, pairs, 0)
    target = jnp.where(is_live, pairs, code_blocks)
    item_split_cols = item_columns.reshape(embedding_width, item_blocks, BLOCK)
    code_column_splits = code_cols.reshape(embedding_width, code_blocks, BLOCK)
    group = math.gcd(item_blocks, 8)
    group_count = item_blocks // group

    def build_tiles(own, ids, live):
        picked = code_column_splits[:, ids, :]
        scores = (
            jnp.einsum("rbi,rbsj->bsij", own, picked, precision=lax.Precision.HIGHEST) * logit_scale
        )
        return jnp.where(live[:, :, None, None], scores, masked_score)

    reduce_fn = lambda tiles, ids, portion: tiles

    def one_group(group_index):
        start = group_index * group
        own = lax.dynamic_slice_in_dim(item_split_cols, start, group, 1)
        ids = lax.dynamic_slice_in_dim(safe_ids, start, group, 0)
        live = lax.dynamic_slice_in_dim(is_live, start, group, 0)
        portion = lax.dynamic_slice_in_dim(safe_ids, start, group, 0)
        return reduce_fn(build_tiles(own, ids, live), ids, portion)

    results = lax.map(one_group, jnp.arange(group_count, dtype=jnp.int32))
    saved_tile_blocks = results.reshape((item_blocks,) + results.shape[2:])

    def run_pass(reduce_fn, extra):
        return reduce_fn(saved_tile_blocks, safe_ids, extra)

    flat_target = target.reshape(-1)
    flat_rows = flat_target.shape[0]
    row_group = math.gcd(flat_rows, 256)
    one_hot = flat_target[:, None] == jnp.arange(code_blocks, dtype=jnp.int32)[None, :]
    one_hot_groups = one_hot.reshape(flat_rows // row_group, row_group, code_blocks)
    one_hot_float = one_hot.astype(jnp.float32)
    code_potential = jnp.zeros((code_count,), jnp.float32)
    item_potential = jnp.zeros((item_count,), jnp.float32)
    for sweep in range(ITERS):
        code_split = code_potential.reshape(code_blocks, BLOCK)

        def row_reduce(tiles, ids, portion):
            logits = tiles + code_split[ids][:, :, None, :]
            block_peak = jnp.max(logits, axis=(1, 3))
            block_total = jnp.sum(jnp.exp(logits - block_peak[:, None, :, None]), axis=(1, 3))
            return (block_peak, block_total)

        row_peak, row_total = run_pass(row_reduce, safe_ids)
        row_peak = row_peak.reshape(item_count)
        row_total = row_total.reshape(item_count)
        merged_peak = lax.pmax(row_peak, "code")
        merged_total = lax.psum(row_total * jnp.exp(row_peak - merged_peak), "code")
        item_potential = item_logmass - (merged_peak + jnp.log(merged_total))
        item_split = item_potential.reshape(item_blocks, BLOCK)

        def col_reduce(tiles, ids, portion):
            logits = tiles + portion[:, None, :, None]
            block_peak = jnp.max(logits, axis=2)
            block_total = jnp.sum(jnp.exp(logits - block_peak[:, :, None, :]), axis=2)
            return (block_peak, block_total)

        tile_peak, tile_total = run_pass(col_reduce, item_split)
        peak_flat = tile_peak.reshape(flat_rows, BLOCK)
        total_flat = tile_total.reshape(flat_rows, BLOCK)
        peak_groups = peak_flat.reshape(flat_rows // row_group, row_group, BLOCK)

        def peak_step(carry, pieces):
            hot, peaks = pieces
            candidate = jnp.max(jnp.where(hot[:, :, None], peaks[:, None, :], masked_score), axis=0)
            return (jnp.maximum(carry, candidate), None)

        col_peak, unused = lax.scan(
            peak_step,
            jnp.full((code_blocks, BLOCK), masked_score, jnp.float32),
            (one_hot_groups, peak_groups),
        )
        padded_peak = jnp.concatenate(
            [col_peak, jnp.full((1, BLOCK), masked_score, jnp.float32)], axis=0
        )
        spread = total_flat * jnp.exp(peak_flat - padded_peak[flat_target])
        col_total = jnp.dot(
            one_hot_float.T,
            spread,
            precision=lax.Precision.HIGHEST,
            preferred_element_type=jnp.float32,
        )
        col_peak = col_peak.reshape(code_count)
        col_total = col_total.reshape(code_count)
        joined_peak = lax.pmax(col_peak, "item")
        joined_total = lax.psum(col_total * jnp.exp(col_peak - joined_peak), "item")
        code_potential = code_logmass - (joined_peak + jnp.log(joined_total))
    return (item_potential, code_potential)


def solution(mesh):
    placed = (P("code", "item"), P("item", "code"), P("item"), P("code"), P("item", "code"))
    return jax.shard_map(
        body, mesh=mesh, in_specs=placed, out_specs=(P("item"), P("code")), check_vma=False
    )
```

profile of v0, /device:TPU:0, one launch (start us, length us, event | category | flops | bytes accessed | tf_op | source)
XLA Modules:
  0.0 1095.6 jit_solution(9727637983515556993)
XLA Ops:
  10.0 42.6 %psum.56 = f32[]{:T(128)} all-reduce(f32[]{:T(128)} %reduce_sum.72), channel_id=1, replica_groups=mesh['item'=16,'code'=8] {'item'}, use_global_device_ids=true, to_apply=%region_1.0 | all-reduce | flops 1 | bytes 8 | tf_op jit(solution)/shard_map/psum | solution.py:22
  58.9 5.6 copy.31
  64.6 52.7 %all-gather.3.cloned.1.call-done = f32[256,8192]{1,0:T(8,128)} async-done(((f32[16,8192]{1,0:T(8,128)}), f32[256,8192]{1,0:T(8,128)}) %all-gather.3.cloned.1.call-update) | async-done | bytes 8388624 | tf_op jit(solution)/shard_map/all_gather | solution.py:15
  117.3 9.0 copy.30
  126.3 158.7 %while.43 = (s32[]{:T(128)}, f32[8,8,16,64,64]{3,4,2,1,0:T(8,128)}, s32[8]{0:T(128)S(1)}, pred[64,16]{1,0:T(8,128)(4,1)S(1)}, s32[64,16]{1,0:T(8,128)S(1)}, /*in...) while((s32[]{:T(128)}, f32[8,8,16,64,64]{3,4,2,1,0:T(8,128)}, ...), condition=%wide.region_3.0_spmd, body=%wide.region_2.0_spmd.sunk | while | flops 1611662720 | bytes 29892660 | solution.py:51
  127.5 7.7 gather_fusion
  135.2 11.0 bitcast_dynamic-update-slice_fusion.2
  147.3 7.7 gather_fusion
  155.0 11.0 %bitcast_dynamic-update-slice_fusion.2 = f32[8,8,16,64,64]{3,4,2,1,0:T(8,128)} fusion(f32[8,8,16,64,64]{3,4,2,1,0:T(8,128)} %get-tuple-element.327, s32[]{:T(128)} %get-tuple-element.326, f32[256,8,16,64]{0,3,2,1:T(8,128)} %bitcast.84, pred[8,16]{1,0:T(8,128)(4,1)S(1)} %constant_dynamic-slice_fusion.2, f32[256,64,64]{0,2,1:T(8,128)} %get-tuple-element.343, ...), kind=kOutput, calls=%fused_computation.7.clone.1 | convolution fusion | flops 1611661312 | bytes 13107844 | tf_op jit(solution)/shard_map/while/body/eval_jaxpr/rbi,rbsj->bsij/dot_general | solution.py:37
  167.2 7.7 gather_fusion
  174.8 10.9 bitcast_dynamic-update-slice_fusion.2
  187.0 7.7 gather_fusion
  194.7 10.9 bitcast_dynamic-update-slice_fusion.2
  206.8 7.7 gather_fusion
  214.5 11.0 bitcast_dynamic-update-slice_fusion.2
  226.7 7.7 gather_fusion
  234.3 11.0 %bitcast_dynamic-update-slice_fusion.2 = f32[8,8,16,64,64]{3,4,2,1,0:T(8,128)} fusion(f32[8,8,16,64,64]{3,4,2,1,0:T(8,128)} %get-tuple-element.327, s32[]{:T(128)} %get-tuple-element.326, f32[256,8,16,64]{0,3,2,1:T(8,128)} %bitcast.84, pred[8,16]{1,0:T(8,128)(4,1)S(1)} %constant_dynamic-slice_fusion.2, f32[256,64,64]{0,2,1:T(8,128)} %get-tuple-element.343, ...), kind=kOutput, calls=%fused_computation.7.clone.1 | convolution fusion | flops 1611661312 | bytes 13107844 | tf_op jit(solution)/shard_map/while/body/eval_jaxpr/rbi,rbsj->bsij/dot_general | solution.py:37
  246.5 7.7 gather_fusion
  254.2 10.9 bitcast_dynamic-update-slice_fusion.2
  266.3 7.7 gather_fusion
  274.0 11.0 %bitcast_dynamic-update-slice_fusion.2 = f32[8,8,16,64,64]{3,4,2,1,0:T(8,128)} fusion(f32[8,8,16,64,64]{3,4,2,1,0:T(8,128)} %get-tuple-element.327, s32[]{:T(128)} %get-tuple-element.326, f32[256,8,16,64]{0,3,2,1:T(8,128)} %bitcast.84, pred[8,16]{1,0:T(8,128)(4,1)S(1)} %constant_dynamic-slice_fusion.2, f32[256,64,64]{0,2,1:T(8,128)} %get-tuple-element.343, ...), kind=kOutput, calls=%fused_computation.7.clone.1 | convolution fusion | flops 1611661312 | bytes 13107844 | tf_op jit(solution)/shard_map/while/body/eval_jaxpr/rbi,rbsj->bsij/dot_general | solution.py:37
  285.0 11.8 %add_reduce_fusion.5 = f32[8,8,64]{2,1,0:T(8,128)S(1)} fusion(f32[8,8,16,64,64]{3,4,2,1,0:T(8,128)} %get-tuple-element.105, f32[8,8,16,64]{3,2,1,0:T(8,128)S(1)} %bitcast.93), kind=kLoop, calls=%fused_computation.37 | loop fusion | flops 8384512 | bytes 17055744 | tf_op jit(solution)/shard_map/reduce_max | solution.py:70
  296.8 11.9 %exponential_reduce_fusion.5 = f32[8,8,64]{2,1,0:T(8,128)S(1)} fusion(f32[8,8,16,64,64]{3,4,2,1,0:T(8,128)} %get-tuple-element.105, f32[8,8,64]{2,1,0:T(8,128)S(1)} %add_reduce_fusion.5, f32[8,8,16,64]{3,2,1,0:T(8,128)S(1)} %bitcast.94), kind=kLoop, calls=%fused_computation.31 | loop fusion | flops 12578816 | bytes 17072128 | tf_op jit(solution)/shard_map/reduce_sum | solution.py:71
  308.9 25.5 %pmax.42 = f32[4096]{0:T(1024)S(1)} all-reduce(f32[4096]{0:T(1024)S(1)} %reshape.211), channel_id=1, replica_groups=mesh['item'=16,'code'=8] {'code'}, use_global_device_ids=true, to_apply=%region_7.8 | all-reduce | flops 4096 | bytes 32768 | tf_op jit(solution)/shard_map/pmax | solution.py:77
  334.4 24.6 %all-reduce.3 = (f32[4096]{0:T(1024)S(1)}, f32[]{:T(128)}) all-reduce(f32[4096]{0:T(1024)S(1)} %exponential_multiply_fusion.5, f32[]{:T(128)} %reduce_sum.73), channel_id=1, replica_groups=mesh['item'=16,'code'=8] {'code'}, use_global_device_ids=true, to_apply=%region_9.10 | all-reduce | flops 4097 | bytes 32776 | tf_op jit(solution)/shard_map/psum | solution.py:78
  359.1 15.3 %add_reduce_fusion.4 = f32[8,8,16,64]{3,2,1,0:T(8,128)S(1)} fusion(f32[8,8,16,64,64]{3,4,2,1,0:T(8,128)} %get-tuple-element.105, f32[8,8,64]{2,1,0:T(8,128)S(1)} %add.154), kind=kLoop, calls=%fused_computation.36 | loop fusion | flops 8323072 | bytes 17055744 | tf_op jit(solution)/shard_map/reduce_max | solution.py:84
  374.4 20.7 %exponential_reduce_fusion.4 = f32[8,8,16,64]{3,2,1,0:T(8,128)S(1)} fusion(f32[8,8,16,64,64]{3,4,2,1,0:T(8,128)} %get-tuple-element.105, f32[8,8,16,64]{3,2,1,0:T(8,128)S(1)} %add_reduce_fusion.4, f32[8,8,64]{2,1,0:T(8,128)S(1)} %add.154), kind=kLoop, calls=%fused_computation.30 | loop fusion | flops 12517376 | bytes 17317888 | tf_op jit(solution)/shard_map/reduce_sum | solution.py:85
  395.1 13.3 %while.44 = (s32[]{:T(128)}, f32[128,64]{0,1:T(8,128)S(1)}, pred[4,256,128]{2,1,0:T(8,128)(4,1)S(1)}, f32[4,256,64]{2,1,0:T(8,128)S(1)}, s32[]{:T(128)}, /*index=5*/s32[]{:T(128)}) while((s32[]{:T(128)}, f32[128,64]{0,1:T(8,128)S(1)}, pred[4,256,128]{2,1,0:T(8,128)(4,1)S(1)}, f32[4,256,64]{2,1,0:T(8,128)S(1)}, s32[]{:T(128)}, ...), condition=%wide.region_13.14_spmd.clone, body=%wide.region_11.13_spmd.clone.sunk | while | flops 4202499 | bytes 426071 | solution.py:98
  412.4 72.4 %pmax.43 = f32[8192]{0:T(1024)S(1)} all-reduce(f32[8192]{0:T(1024)S(1)} %reshape.213), channel_id=1, replica_groups=mesh['item'=16,'code'=8] {'item'}, use_global_device_ids=true, to_apply=%region_14.15 | all-reduce | flops 8192 | bytes 65536 | tf_op jit(solution)/shard_map/pmax | solution.py:115
  484.8 69.5 %psum.59 = f32[8192]{0:T(1024)S(1)} all-reduce(f32[8192]{0:T(1024)S(1)} %exponential_multiply_fusion.2), channel_id=1, replica_groups=mesh['item'=16,'code'=8] {'item'}, use_global_device_ids=true, to_apply=%region_16.17 | all-reduce | flops 8192 | bytes 65536 | tf_op jit(solution)/shard_map/psum | solution.py:116
  558.0 11.8 %add_reduce_fusion.3 = f32[8,8,64]{2,1,0:T(8,128)S(1)} fusion(f32[8,8,16,64,64]{3,4,2,1,0:T(8,128)} %get-tuple-element.105, f32[8,8,16,64]{3,2,1,0:T(8,128)S(1)} %bitcast.97), kind=kLoop, calls=%fused_computation.35 | loop fusion | flops 8384512 | bytes 17055744 | tf_op jit(solution)/shard_map/reduce_max | solution.py:70
  569.8 11.9 %exponential_reduce_fusion.3 = f32[8,8,64]{2,1,0:T(8,128)S(1)} fusion(f32[8,8,16,64,64]{3,4,2,1,0:T(8,128)} %get-tuple-element.105, f32[8,8,64]{2,1,0:T(8,128)S(1)} %add_reduce_fusion.3, f32[8,8,16,64]{3,2,1,0:T(8,128)S(1)} %bitcast.98), kind=kLoop, calls=%fused_computation.29 | loop fusion | flops 12578816 | bytes 17072128 | tf_op jit(solution)/shard_map/reduce_sum | solution.py:71
  581.9 23.5 %pmax.44 = f32[4096]{0:T(1024)S(1)} all-reduce(f32[4096]{0:T(1024)S(1)} %reshape.219), channel_id=1, replica_groups=mesh['item'=16,'code'=8] {'code'}, use_global_device_ids=true, to_apply=%region_18.19 | all-reduce | flops 4096 | bytes 32768 | tf_op jit(solution)/shard_map/pmax | solution.py:77
  605.4 23.6 %psum.60 = f32[4096]{0:T(1024)S(1)} all-reduce(f32[4096]{0:T(1024)S(1)} %exponential_multiply_fusion.4), channel_id=1, replica_groups=mesh['item'=16,'code'=8] {'code'}, use_global_device_ids=true, to_apply=%region_20.21 | all-reduce | flops 4096 | bytes 32768 | tf_op jit(solution)/shard_map/psum | solution.py:78
  629.1 15.3 %add_reduce_fusion.2 = f32[8,8,16,64]{3,2,1,0:T(8,128)S(1)} fusion(f32[8,8,16,64,64]{3,4,2,1,0:T(8,128)} %get-tuple-element.105, f32[8,8,64]{2,1,0:T(8,128)S(1)} %add.163), kind=kLoop, calls=%fused_computation.34 | loop fusion | flops 8323072 | bytes 17055744 | tf_op jit(solution)/shard_map/reduce_max | solution.py:84
  644.4 20.7 %exponential_reduce_fusion.2 = f32[8,8,16,64]{3,2,1,0:T(8,128)S(1)} fusion(f32[8,8,16,64,64]{3,4,2,1,0:T(8,128)} %get-tuple-element.105, f32[8,8,16,64]{3,2,1,0:T(8,128)S(1)} %add_reduce_fusion.2, f32[8,8,64]{2,1,0:T(8,128)S(1)} %add.163), kind=kLoop, calls=%fused_computation.28 | loop fusion | flops 12517376 | bytes 17317888 | tf_op jit(solution)/shard_map/reduce_sum | solution.py:85
  665.0 13.3 %while.45 = (s32[]{:T(128)}, f32[128,64]{0,1:T(8,128)S(1)}, pred[4,256,128]{2,1,0:T(8,128)(4,1)S(1)}, f32[4,256,64]{2,1,0:T(8,128)S(1)}, s32[]{:T(128)}, /*index=5*/s32[]{:T(128)}) while((s32[]{:T(128)}, f32[128,64]{0,1:T(8,128)S(1)}, pred[4,256,128]{2,1,0:T(8,128)(4,1)S(1)}, f32[4,256,64]{2,1,0:T(8,128)S(1)}, s32[]{:T(128)}, ...), condition=%wide.region_24.25_spmd.clone, body=%wide.region_22.24_spmd.clone.sunk | while | flops 4202499 | bytes 426071 | solution.py:98
  682.3 69.6 %pmax.45 = f32[8192]{0:T(1024)S(1)} all-reduce(f32[8192]{0:T(1024)S(1)} %reshape.221), channel_id=1, replica_groups=mesh['item'=16,'code'=8] {'item'}, use_global_device_ids=true, to_apply=%region_25.26 | all-reduce | flops 8192 | bytes 65536 | tf_op jit(solution)/shard_map/pmax | solution.py:115
  751.9 69.5 %psum.61 = f32[8192]{0:T(1024)S(1)} all-reduce(f32[8192]{0:T(1024)S(1)} %exponential_multiply_fusion.1), channel_id=1, replica_groups=mesh['item'=16,'code'=8] {'item'}, use_global_device_ids=true, to_apply=%region_27.28 | all-reduce | flops 8192 | bytes 65536 | tf_op jit(solution)/shard_map/psum | solution.py:116
  824.4 11.8 %add_reduce_fusion.1 = f32[8,8,64]{2,1,0:T(8,128)S(1)} fusion(f32[8,8,16,64,64]{3,4,2,1,0:T(8,128)} %get-tuple-element.105, f32[8,8,16,64]{3,2,1,0:T(8,128)S(1)} %bitcast.95), kind=kLoop, calls=%fused_computation.33 | loop fusion | flops 8384512 | bytes 17055744 | tf_op jit(solution)/shard_map/reduce_max | solution.py:70
  836.2 11.9 %exponential_reduce_fusion.1 = f32[8,8,64]{2,1,0:T(8,128)S(1)} fusion(f32[8,8,16,64,64]{3,4,2,1,0:T(8,128)} %get-tuple-element.105, f32[8,8,64]{2,1,0:T(8,128)S(1)} %add_reduce_fusion.1, f32[8,8,16,64]{3,2,1,0:T(8,128)S(1)} %bitcast.96), kind=kLoop, calls=%fused_computation.27 | loop fusion | flops 12578816 | bytes 17072128 | tf_op jit(solution)/shard_map/reduce_sum | solution.py:71
  848.3 23.5 %pmax.46 = f32[4096]{0:T(1024)S(1)} all-reduce(f32[4096]{0:T(1024)S(1)} %reshape.226), channel_id=1, replica_groups=mesh['item'=16,'code'=8] {'code'}, use_global_device_ids=true, to_apply=%region_29.30 | all-reduce | flops 4096 | bytes 32768 | tf_op jit(solution)/shard_map/pmax | solution.py:77
  871.8 23.8 %psum.62 = f32[4096]{0:T(1024)S(1)} all-reduce(f32[4096]{0:T(1024)S(1)} %exponential_multiply_fusion.3), channel_id=1, replica_groups=mesh['item'=16,'code'=8] {'code'}, use_global_device_ids=true, to_apply=%region_31.32 | all-reduce | flops 4096 | bytes 32768 | tf_op jit(solution)/shard_map/psum | solution.py:78
  895.7 15.3 %add_reduce_fusion = f32[8,8,16,64]{3,2,1,0:T(8,128)S(1)} fusion(f32[8,8,16,64,64]{3,4,2,1,0:T(8,128)} %get-tuple-element.105, f32[8,8,64]{2,1,0:T(8,128)S(1)} %add.171), kind=kLoop, calls=%fused_computation.32 | loop fusion | flops 8323072 | bytes 17055744 | tf_op jit(solution)/shard_map/reduce_max | solution.py:84
  911.0 20.7 %exponential_reduce_fusion = f32[8,8,16,64]{3,2,1,0:T(8,128)S(1)} fusion(f32[8,8,16,64,64]{3,4,2,1,0:T(8,128)} %get-tuple-element.105, f32[8,8,16,64]{3,2,1,0:T(8,128)S(1)} %add_reduce_fusion, f32[8,8,64]{2,1,0:T(8,128)S(1)} %add.171), kind=kLoop, calls=%fused_computation.26 | loop fusion | flops 12517376 | bytes 17317888 | tf_op jit(solution)/shard_map/reduce_sum | solution.py:85
  931.7 13.3 %while.46 = (s32[]{:T(128)}, f32[128,64]{0,1:T(8,128)S(1)}, pred[4,256,128]{2,1,0:T(8,128)(4,1)S(1)}, f32[4,256,64]{2,1,0:T(8,128)S(1)}, s32[]{:T(128)}, /*index=5*/s32[]{:T(128)}) while((s32[]{:T(128)}, f32[128,64]{0,1:T(8,128)S(1)}, pred[4,256,128]{2,1,0:T(8,128)(4,1)S(1)}, f32[4,256,64]{2,1,0:T(8,128)S(1)}, s32[]{:T(128)}, ...), condition=%wide.region_35.36_spmd.clone, body=%wide.region_33.35_spmd.clone.sunk | while | flops 4202499 | bytes 426071 | solution.py:98
  948.9 69.6 %pmax.47 = f32[8192]{0:T(1024)S(1)} all-reduce(f32[8192]{0:T(1024)S(1)} %reshape.228), channel_id=1, replica_groups=mesh['item'=16,'code'=8] {'item'}, use_global_device_ids=true, to_apply=%region_36.37 | all-reduce | flops 8192 | bytes 65536 | tf_op jit(solution)/shard_map/pmax | solution.py:115
  1018.5 69.5 %psum.63 = f32[8192]{0:T(1024)S(1)} all-reduce(f32[8192]{0:T(1024)S(1)} %exponential_multiply_fusion), channel_id=1, replica_groups=mesh['item'=16,'code'=8] {'item'}, use_global_device_ids=true, to_apply=%region_38.39 | all-reduce | flops 8192 | bytes 65536 | tf_op jit(solution)/shard_map/psum | solution.py:116
  (169 shorter events, 71.9 us)
Async XLA Ops:
  7.2 51.8 %all-gather.5.cloned.1.call-start = ((), (), s32[]{:S(2)}) async-start(), calls=%async_computation.1 | async-start | bytes 4718592 | tf_op jit(solution)/shard_map/all_gather | solution.py:14
  7.9 109.4 %all-gather.3.cloned.1.call-start = ((), (), s32[]{:S(2)}) async-start(), calls=%async_computation | async-start | bytes 8912896 | tf_op jit(solution)/shard_map/all_gather | solution.py:15
  285.0 74.0 %copy-start.3 = (f32[4096]{0:T(1024)S(1)}, f32[4096]{0:T(1024)}, u32[]{:S(2)}) copy-start(f32[4096]{0:T(1024)} %param.15) | copy-start | bytes 49156
  359.1 195.9 %copy-start.2 = (f32[8192]{0:T(1024)S(1)}, f32[8192]{0:T(1024)}, u32[]{:S(2)}) copy-start(f32[8192]{0:T(1024)} %param.16) | copy-start | bytes 98308
  629.1 36.0 %copy-start.1 = (f32[128,64]{0,1:T(8,128)S(1)}, f32[128,64]{0,1:T(8,128)}, u32[]{:S(2)}) copy-start(f32[128,64]{0,1:T(8,128)} %custom-call.1) | copy-start | bytes 98308
  895.6 36.1 %copy-start.4 = (f32[4096]{0:T(1024)}, f32[4096]{0:T(1024)S(1)}, u32[]{:S(2)}) copy-start(f32[4096]{0:T(1024)S(1)} %add_subtract_fusion.3) | copy-start | bytes 49156
  895.7 36.0 %copy-start = (f32[128,64]{0,1:T(8,128)S(1)}, f32[128,64]{0,1:T(8,128)}, u32[]{:S(2)}) copy-start(f32[128,64]{0,1:T(8,128)} %custom-call.2) | copy-start | bytes 98308
Sparse Core Ops, SparseCore 0:
  9.7 34.5 all-gather.4
  46.4 70.8 all-gather.2
where the time goes:
time: 1100 us
  blocking collectives  607 us (55%)
  other arithmetic  222 us (20%)
  local copies, waits for them, and re-layouts  101 us (9%)
  matrix products  89.9 us (8%)
  waiting for transfers between devices  54.1 us (5%)
  between operations  15.8 us (1%)
    pmax x3, blocking collectives, body(): joined_peak = lax.pmax(col_peak, 'item')  212 us
    psum x3, blocking collectives, body(): joined_total = lax.psum(col_total * jnp.exp(col_peak - joined_peak), 'item')  209 us
    dot_general x8, matrix products, build_tiles(): jnp.einsum('rbi,rbsj->bsij', own, picked, precision=lax.Precision.HIGHEST)  87.6 us
    pmax x3, blocking collectives, body(): merged_peak = lax.pmax(row_peak, 'code')  72.6 us
    psum x3, blocking collectives, body(): merged_total = lax.psum(row_total * jnp.exp(row_peak - merged_peak), 'code')  71.9 us
    reduce_sum x3, other arithmetic, col_reduce(): block_total = jnp.sum(jnp.exp(logits - block_peak[:, :, None, :]), axis=2)  62 us
    gather x8, local copies, waits for them, and re-layouts, build_tiles(): picked = code_column_splits[:, ids, :]  61.3 us
    all_gather x1, waiting for transfers between devices, body(): code_cols = lax.all_gather(codebook, 'item', axis=0, tiled=True)  52.7 us
  transfers between devices with their start and end apart: 2, of which 1 were waited for; matrix products, arithmetic and copies ran while one was open for 1% of the time, Pallas kernels for 0%

commit v1 on v0

--- a/solution.py
+++ b/solution.py
@@ -12,7 +12,26 @@
 
 def body(residuals, codebook, item_weight, code_capacity, pairs):
     item_columns = lax.all_gather(residuals, "code", axis=0, tiled=True)
-    code_cols = lax.all_gather(codebook, "item", axis=0, tiled=True)
+    peers, index, width = (lax.axis_size("item"), lax.axis_index("item"), codebook.shape[0])
+    ahead = [(i, (i + 1) % peers) for i in range(peers)]
+    backward = [(i, (i - 1) % peers) for i in range(peers)]
+    filled = jnp.zeros(
+        (*codebook.shape[:0], peers * width, *codebook.shape[0 + 1 :]), codebook.dtype
+    )
+    filled = lax.dynamic_update_slice_in_dim(filled, codebook, index * width, axis=0)
+    from_left = from_right = codebook
+    half = peers // 2
+    for step in range(1, half + 1):
+        from_left = lax.ppermute(from_left, "item", ahead)
+        filled = lax.dynamic_update_slice_in_dim(
+            filled, from_left, (index - step) % peers * width, axis=0
+        )
+        if step < peers - half:
+            from_right = lax.ppermute(from_right, "item", backward)
+            filled = lax.dynamic_update_slice_in_dim(
+                filled, from_right, (index + step) % peers * width, axis=0
+            )
+    code_cols = filled
     embedding_width = item_columns.shape[0]
     item_count = item_columns.shape[1]
     code_count = code_cols.shape[1]

time: 1100 us -> 1570 us (1.43)
  local copies, waits for them, and re-layouts: 101 us -> 520 us
  starting transfers between devices: 0.08 us -> 37.5 us
    dynamic_update_slice x0 -> x16, local copies, waits for them, and re-layouts: none -> 375 us  [the longest x8 184 us: body(): lax.dynamic_update_slice_in_dim(filled, from_left, (index - step) % peers...]
    ppermute x0 -> x15, waiting for transfers between devices: none -> 63.6 us  [the longest x8 63.6 us: body(): from_left = lax.ppermute(from_left, 'item', ahead)]
    all_gather x1 -> x0, waiting for transfers between devices: 52.7 us -> none  [body(): code_cols = lax.all_gather(codebook, 'item', axis=0, tiled=True)]
    ppermute x0 -> x15, local copies, waits for them, and re-layouts: none -> 43.6 us  [the longest x8 22.6 us: body(): from_left = lax.ppermute(from_left, 'item', ahead)]
    ppermute x0 -> x15, starting transfers between devices: none -> 37.5 us  [the longest x7 35.7 us: body(): from_right = lax.ppermute(from_right, 'item', backward)]
  transfers between devices with their start and end apart: 2 -> 16, of which waited for: 1 -> 7; matrix products, arithmetic and copies ran while one was open for 1% -> 28% of each run, Pallas kernels for 0% -> 0%
where the time goes in v1:
time: 1570 us; the launch traced here: 1560 us
  blocking collectives  602 us (38%)
  local copies, waits for them, and re-layouts  520 us (33%)
  other arithmetic  224 us (14%)
  matrix products  89.9 us (6%)
  waiting for transfers between devices  64.3 us (4%)
  starting transfers between devices  37.5 us (2%)
  between operations  16.2 us (1%)
    psum x3, blocking collectives, body(): joined_total = lax.psum(col_total * jnp.exp(col_peak - joined_peak), 'item')  209 us
    pmax x3, blocking collectives, body(): joined_peak = lax.pmax(col_peak, 'item')  209 us
    dynamic_update_slice x8, local copies, waits for them, and re-layouts, body(): lax.dynamic_update_slice_in_dim(filled, from_left, (index - step) % peers...  184 us
    dynamic_update_slice x7, local copies, waits for them, and re-layouts, body(): lax.dynamic_update_slice_in_dim(filled, from_right, (index + step) % peer...  170 us
    dot_general x8, matrix products, build_tiles(): jnp.einsum('rbi,rbsj->bsij', own, picked, precision=lax.Precision.HIGHEST)  87.6 us
    psum x3, blocking collectives, body(): merged_total = lax.psum(row_total * jnp.exp(row_peak - merged_peak), 'code')  72 us
    pmax x3, blocking collectives, body(): merged_peak = lax.pmax(row_peak, 'code')  70.6 us
    ppermute x8, waiting for transfers between devices, body(): from_left = lax.ppermute(from_left, 'item', ahead)  63.6 us
  transfers between devices with their start and end apart: 16, of which 7 were waited for; matrix products, arithmetic and copies ran while one was open for 28% of the time, Pallas kernels for 0%

profile of v1, /device:TPU:0, one launch (start us, length us, event | category | flops | bytes accessed | tf_op | source)
XLA Modules:
  0.0 1559.2 jit_solution(5130218817349166997)
XLA Ops:
  14.6 12.1 collective-permute-done
  32.0 11.1 collective-permute-done.2
  113.5 41.7 %psum.56 = f32[]{:T(128)} all-reduce(f32[]{:T(128)} %reduce_sum.72), channel_id=1, replica_groups=mesh['item'=16,'code'=8] {'item'}, use_global_device_ids=true, to_apply=%region_1.2 | all-reduce | flops 1 | bytes 8 | tf_op jit(solution)/shard_map/psum | solution.py:41
  168.3 21.2 %dynamic_update_slice.52 = f32[256,8192]{0,1:T(8,128)} dynamic-update-slice(f32[256,8192]{0,1:T(8,128)} %broadcast_in_dim.114, f32[16,8192]{0,1:T(8,128)} %copy.47, s32[]{:T(128)S(6)} %select_n.161, s32[]{:T(128)} %constant.156.clone.1) | dynamic-update-slice | bytes 1048580 | tf_op jit(solution)/shard_map/dynamic_update_slice | solution.py:21
  192.9 23.4 %dynamic_update_slice.53 = f32[256,8192]{0,1:T(8,128)} dynamic-update-slice(f32[256,8192]{0,1:T(8,128)} %dynamic_update_slice.52, f32[16,8192]{0,1:T(8,128)} %copy.48, s32[]{:T(128)S(6)} %select_n.163, s32[]{:T(128)} %constant.156.clone.1) | dynamic-update-slice | bytes 1048580 | tf_op jit(solution)/shard_map/dynamic_update_slice | solution.py:26
  218.9 24.3 %dynamic_update_slice.54 = f32[256,8192]{0,1:T(8,128)} dynamic-update-slice(f32[256,8192]{0,1:T(8,128)} %dynamic_update_slice.53, f32[16,8192]{0,1:T(8,128)} %copy.49, s32[]{:T(128)S(6)} %select_n.165, s32[]{:T(128)} %constant.156.clone.1) | dynamic-update-slice | bytes 1048580 | tf_op jit(solution)/shard_map/dynamic_update_slice | solution.py:31
  245.8 23.4 %dynamic_update_slice.55 = f32[256,8192]{0,1:T(8,128)} dynamic-update-slice(f32[256,8192]{0,1:T(8,128)} %dynamic_update_slice.54, f32[16,8192]{0,1:T(8,128)} %copy.50, s32[]{:T(128)S(6)} %select_n.167, s32[]{:T(128)} %constant.156.clone.1) | dynamic-update-slice | bytes 1048580 | tf_op jit(solution)/shard_map/dynamic_update_slice | solution.py:26
  271.9 24.3 %dynamic_update_slice.56 = f32[256,8192]{0,1:T(8,128)} dynamic-update-slice(f32[256,8192]{0,1:T(8,128)} %dynamic_update_slice.55, f32[16,8192]{0,1:T(8,128)} %copy.51, s32[]{:T(128)S(6)} %select_n.169, s32[]{:T(128)} %constant.156.clone.1) | dynamic-update-slice | bytes 1048580 | tf_op jit(solution)/shard_map/dynamic_update_slice | solution.py:31
  298.8 23.4 %dynamic_update_slice.57 = f32[256,8192]{0,1:T(8,128)} dynamic-update-slice(f32[256,8192]{0,1:T(8,128)} %dynamic_update_slice.56, f32[16,8192]{0,1:T(8,128)} %copy.52, s32[]{:T(128)S(6)} %select_n.171, s32[]{:T(128)} %constant.156.clone.1) | dynamic-update-slice | bytes 1048580 | tf_op jit(solution)/shard_map/dynamic_update_slice | solution.py:26
  324.8 24.3 %dynamic_update_slice.58 = f32[256,8192]{0,1:T(8,128)} dynamic-update-slice(f32[256,8192]{0,1:T(8,128)} %dynamic_update_slice.57, f32[16,8192]{0,1:T(8,128)} %copy.53, s32[]{:T(128)S(6)} %select_n.173, s32[]{:T(128)} %constant.156.clone.1) | dynamic-update-slice | bytes 1048580 | tf_op jit(solution)/shard_map/dynamic_update_slice | solution.py:31
  351.8 23.4 %dynamic_update_slice.59 = f32[256,8192]{0,1:T(8,128)} dynamic-update-slice(f32[256,8192]{0,1:T(8,128)} %dynamic_update_slice.58, f32[16,8192]{0,1:T(8,128)} %copy.54, s32[]{:T(128)S(6)} %select_n.175, s32[]{:T(128)} %constant.156.clone.1) | dynamic-update-slice | bytes 1048580 | tf_op jit(solution)/shard_map/dynamic_update_slice | solution.py:26
  377.8 24.3 %dynamic_update_slice.60 = f32[256,8192]{0,1:T(8,128)} dynamic-update-slice(f32[256,8192]{0,1:T(8,128)} %dynamic_update_slice.59, f32[16,8192]{0,1:T(8,128)} %copy.55, s32[]{:T(128)S(6)} %select_n.177, s32[]{:T(128)} %constant.156.clone.1) | dynamic-update-slice | bytes 1048580 | tf_op jit(solution)/shard_map/dynamic_update_slice | solution.py:31
  404.6 23.4 %dynamic_update_slice.61 = f32[256,8192]{0,1:T(8,128)} dynamic-update-slice(f32[256,8192]{0,1:T(8,128)} %dynamic_update_slice.60, f32[16,8192]{0,1:T(8,128)} %copy.56, s32[]{:T(128)S(6)} %select_n.179, s32[]{:T(128)} %constant.156.clone.1) | dynamic-update-slice | bytes 1048580 | tf_op jit(solution)/shard_map/dynamic_update_slice | solution.py:26
  431.5 24.3 %dynamic_update_slice.62 = f32[256,8192]{0,1:T(8,128)} dynamic-update-slice(f32[256,8192]{0,1:T(8,128)} %dynamic_update_slice.61, f32[16,8192]{0,1:T(8,128)} %copy.57, s32[]{:T(128)S(6)} %select_n.181, s32[]{:T(128)} %constant.156.clone.1) | dynamic-update-slice | bytes 1048580 | tf_op jit(solution)/shard_map/dynamic_update_slice | solution.py:31
  459.3 23.4 %dynamic_update_slice.63 = f32[256,8192]{0,1:T(8,128)} dynamic-update-slice(f32[256,8192]{0,1:T(8,128)} %dynamic_update_slice.62, f32[16,8192]{0,1:T(8,128)} %copy.58, s32[]{:T(128)S(6)} %select_n.183, s32[]{:T(128)} %constant.156.clone.1) | dynamic-update-slice | bytes 1048580 | tf_op jit(solution)/shard_map/dynamic_update_slice | solution.py:26
  486.2 24.3 %dynamic_update_slice.64 = f32[256,8192]{0,1:T(8,128)} dynamic-update-slice(f32[256,8192]{0,1:T(8,128)} %dynamic_update_slice.63, f32[16,8192]{0,1:T(8,128)} %copy.59, s32[]{:T(128)S(6)} %select_n.185, s32[]{:T(128)} %constant.156.clone.1) | dynamic-update-slice | bytes 1048580 | tf_op jit(solution)/shard_map/dynamic_update_slice | solution.py:31
  513.0 23.4 %dynamic_update_slice.65 = f32[256,8192]{0,1:T(8,128)} dynamic-update-slice(f32[256,8192]{0,1:T(8,128)} %dynamic_update_slice.64, f32[16,8192]{0,1:T(8,128)} %copy.60, s32[]{:T(128)S(6)} %select_n.187, s32[]{:T(128)} %constant.156.clone.1) | dynamic-update-slice | bytes 1048580 | tf_op jit(solution)/shard_map/dynamic_update_slice | solution.py:26
  539.9 24.3 %dynamic_update_slice.66 = f32[256,8192]{0,1:T(8,128)} dynamic-update-slice(f32[256,8192]{0,1:T(8,128)} %dynamic_update_slice.65, f32[16,8192]{0,1:T(8,128)} %copy.61, s32[]{:T(128)S(6)} %select_n.189, s32[]{:T(128)} %constant.156.clone.1) | dynamic-update-slice | bytes 1048580 | tf_op jit(solution)/shard_map/dynamic_update_slice | solution.py:31
  567.7 20.1 %dynamic_update_slice.67 = f32[256,8192]{0,1:T(8,128)} dynamic-update-slice(f32[256,8192]{0,1:T(8,128)} %dynamic_update_slice.66, f32[16,8192]{0,1:T(8,128)} %copy.62, s32[]{:T(128)S(6)} %select_n.191, s32[]{:T(128)} %constant.156.clone.1) | dynamic-update-slice | bytes 1048580 | tf_op jit(solution)/shard_map/dynamic_update_slice | solution.py:26
  593.5 159.4 %while.43 = (s32[]{:T(128)}, f32[8,8,16,64,64]{3,4,2,1,0:T(8,128)}, s32[8]{0:T(128)S(1)}, pred[64,16]{1,0:T(8,128)(4,1)S(1)}, s32[64,16]{1,0:T(8,128)S(1)}, /*in...) while((s32[]{:T(128)}, f32[8,8,16,64,64]{3,4,2,1,0:T(8,128)}, ...), condition=%wide.region_3.4_spmd, body=%wide.region_2.3_spmd.sunk | while | flops 1611662720 | bytes 29892660 | solution.py:70
  622.8 11.0 bitcast_dynamic-update-slice_fusion.2
  752.9 11.8 add_reduce_fusion.5
  764.7 11.9 exponential_reduce_fusion.5
  776.8 23.5 %pmax.42 = f32[4096]{0:T(1024)S(1)} all-reduce(f32[4096]{0:T(1024)S(1)} %reshape.211), channel_id=1, replica_groups=mesh['item'=16,'code'=8] {'code'}, use_global_device_ids=true, to_apply=%region_7.8 | all-reduce | flops 4096 | bytes 32768 | tf_op jit(solution)/shard_map/pmax | solution.py:96
  800.3 24.7 %all-reduce.3 = (f32[4096]{0:T(1024)S(1)}, f32[]{:T(128)}) all-reduce(f32[4096]{0:T(1024)S(1)} %exponential_multiply_fusion.5, f32[]{:T(128)} %reduce_sum.73), channel_id=1, replica_groups=mesh['item'=16,'code'=8] {'code'}, use_global_device_ids=true, to_apply=%region_9.10 | all-reduce | flops 4097 | bytes 32776 | tf_op jit(solution)/shard_map/psum | solution.py:97
  825.1 15.3 add_reduce_fusion.4
  840.5 20.7 %exponential_reduce_fusion.4 = f32[8,8,16,64]{3,2,1,0:T(8,128)S(1)} fusion(f32[8,8,16,64,64]{3,4,2,1,0:T(8,128)} %get-tuple-element.105, f32[8,8,16,64]{3,2,1,0:T(8,128)S(1)} %add_reduce_fusion.4, f32[8,8,64]{2,1,0:T(8,128)S(1)} %add.315), kind=kLoop, calls=%fused_computation.30 | loop fusion | flops 12517376 | bytes 17317888 | tf_op jit(solution)/shard_map/reduce_sum | solution.py:104
  861.2 13.3 while.44
  878.5 69.5 %pmax.43 = f32[8192]{0:T(1024)S(1)} all-reduce(f32[8192]{0:T(1024)S(1)} %reshape.213), channel_id=1, replica_groups=mesh['item'=16,'code'=8] {'item'}, use_global_device_ids=true, to_apply=%region_14.15 | all-reduce | flops 8192 | bytes 65536 | tf_op jit(solution)/shard_map/pmax | solution.py:134
  948.0 69.7 %psum.59 = f32[8192]{0:T(1024)S(1)} all-reduce(f32[8192]{0:T(1024)S(1)} %exponential_multiply_fusion.2), channel_id=1, replica_groups=mesh['item'=16,'code'=8] {'item'}, use_global_device_ids=true, to_apply=%region_16.17 | all-reduce | flops 8192 | bytes 65536 | tf_op jit(solution)/shard_map/psum | solution.py:135
  1021.3 11.8 add_reduce_fusion.3
  1033.2 11.9 exponential_reduce_fusion.3
  1045.2 23.5 %pmax.44 = f32[4096]{0:T(1024)S(1)} all-reduce(f32[4096]{0:T(1024)S(1)} %reshape.219), channel_id=1, replica_groups=mesh['item'=16,'code'=8] {'code'}, use_global_device_ids=true, to_apply=%region_18.19 | all-reduce | flops 4096 | bytes 32768 | tf_op jit(solution)/shard_map/pmax | solution.py:96
  1068.8 23.6 %psum.60 = f32[4096]{0:T(1024)S(1)} all-reduce(f32[4096]{0:T(1024)S(1)} %exponential_multiply_fusion.4), channel_id=1, replica_groups=mesh['item'=16,'code'=8] {'code'}, use_global_device_ids=true, to_apply=%region_20.21 | all-reduce | flops 4096 | bytes 32768 | tf_op jit(solution)/shard_map/psum | solution.py:97
  1092.4 15.3 add_reduce_fusion.2
  1107.7 20.7 %exponential_reduce_fusion.2 = f32[8,8,16,64]{3,2,1,0:T(8,128)S(1)} fusion(f32[8,8,16,64,64]{3,4,2,1,0:T(8,128)} %get-tuple-element.105, f32[8,8,16,64]{3,2,1,0:T(8,128)S(1)} %add_reduce_fusion.2, f32[8,8,64]{2,1,0:T(8,128)S(1)} %add.324), kind=kLoop, calls=%fused_computation.28 | loop fusion | flops 12517376 | bytes 17317888 | tf_op jit(solution)/shard_map/reduce_sum | solution.py:104
  1128.4 13.3 while.45
  1145.7 69.6 %pmax.45 = f32[8192]{0:T(1024)S(1)} all-reduce(f32[8192]{0:T(1024)S(1)} %reshape.221), channel_id=1, replica_groups=mesh['item'=16,'code'=8] {'item'}, use_global_device_ids=true, to_apply=%region_25.26 | all-reduce | flops 8192 | bytes 65536 | tf_op jit(solution)/shard_map/pmax | solution.py:134
  1215.3 69.5 %psum.61 = f32[8192]{0:T(1024)S(1)} all-reduce(f32[8192]{0:T(1024)S(1)} %exponential_multiply_fusion.1), channel_id=1, replica_groups=mesh['item'=16,'code'=8] {'item'}, use_global_device_ids=true, to_apply=%region_27.28 | all-reduce | flops 8192 | bytes 65536 | tf_op jit(solution)/shard_map/psum | solution.py:135
  1287.7 11.8 add_reduce_fusion.1
  1299.6 11.9 exponential_reduce_fusion.1
  1311.6 23.5 %pmax.46 = f32[4096]{0:T(1024)S(1)} all-reduce(f32[4096]{0:T(1024)S(1)} %reshape.226), channel_id=1, replica_groups=mesh['item'=16,'code'=8] {'code'}, use_global_device_ids=true, to_apply=%region_29.30 | all-reduce | flops 4096 | bytes 32768 | tf_op jit(solution)/shard_map/pmax | solution.py:96
  1335.2 23.8 %psum.62 = f32[4096]{0:T(1024)S(1)} all-reduce(f32[4096]{0:T(1024)S(1)} %exponential_multiply_fusion.3), channel_id=1, replica_groups=mesh['item'=16,'code'=8] {'code'}, use_global_device_ids=true, to_apply=%region_31.32 | all-reduce | flops 4096 | bytes 32768 | tf_op jit(solution)/shard_map/psum | solution.py:97
  1359.1 15.3 add_reduce_fusion
  1374.4 20.7 %exponential_reduce_fusion = f32[8,8,16,64]{3,2,1,0:T(8,128)S(1)} fusion(f32[8,8,16,64,64]{3,4,2,1,0:T(8,128)} %get-tuple-element.105, f32[8,8,16,64]{3,2,1,0:T(8,128)S(1)} %add_reduce_fusion, f32[8,8,64]{2,1,0:T(8,128)S(1)} %add.332), kind=kLoop, calls=%fused_computation.26 | loop fusion | flops 12517376 | bytes 17317888 | tf_op jit(solution)/shard_map/reduce_sum | solution.py:104
  1395.1 13.3 while.46
  1412.3 69.6 %pmax.47 = f32[8192]{0:T(1024)S(1)} all-reduce(f32[8192]{0:T(1024)S(1)} %reshape.228), channel_id=1, replica_groups=mesh['item'=16,'code'=8] {'item'}, use_global_device_ids=true, to_apply=%region_36.37 | all-reduce | flops 8192 | bytes 65536 | tf_op jit(solution)/shard_map/pmax | solution.py:134
  1481.9 69.5 %psum.63 = f32[8192]{0:T(1024)S(1)} all-reduce(f32[8192]{0:T(1024)S(1)} %exponential_multiply_fusion), channel_id=1, replica_groups=mesh['item'=16,'code'=8] {'item'}, use_global_device_ids=true, to_apply=%region_38.39 | all-reduce | flops 8192 | bytes 65536 | tf_op jit(solution)/shard_map/psum | solution.py:135
  (260 shorter events, 347.1 us)
Async XLA Ops:
  7.2 580.7 %all-gather.2.cloned.1.call-start = ((), (), s32[]{:S(2)}) async-start(), calls=%async_computation | async-start | bytes 4718592 | tf_op jit(solution)/shard_map/all_gather | solution.py:14
  7.9 18.8 %collective-permute-start = (f32[16,8192]{1,0:T(8,128)}, f32[16,8192]{1,0:T(8,128)S(1)}, u32[]{:S(2)}, u32[]{:S(2)}) collective-permute-start(f32[16,8192]{1,0:T(8,128)} %param.14), channel_id=1, source_target_pairs={{0,8},{8,16},{16,24},{24,32},{32,40},{40,48},{48,56},{56,64},{64,7... | collective-permute-start | bytes 1572872 | tf_op jit(solution)/shard_map/ppermute | solution.py:25
  9.6 17.1 %collective-permute-start.1 = (f32[16,8192]{1,0:T(8,128)}, f32[16,8192]{1,0:T(8,128)S(1)}, u32[]{:S(2)}, u32[]{:S(2)}) collective-permute-start(f32[16,8192]{1,0:T(8,128)} %param.14), channel_id=1, source_target_pairs={{0,120},{8,0},{16,8},{24,16},{32,24},{40,32},{48,40},{56,48},{64,5... | collective-permute-start | bytes 1572872 | tf_op jit(solution)/shard_map/ppermute | solution.py:30
  26.7 16.4 %collective-permute-start.2 = (f32[16,8192]{1,0:T(8,128)S(1)}, f32[16,8192]{1,0:T(8,128)S(1)}, u32[]{:S(2)}, u32[]{:S(2)}) collective-permute-start(f32[16,8192]{1,0:T(8,128)S(1)} %collective-permute-done), channel_id=1, source_target_pairs={{0,8},{8,16},{16,24},{24,32},{32,40},{40,48},{48,56},{56,64},{64,7... | collective-permute-start | bytes 1572872 | tf_op jit(solution)/shard_map/ppermute | solution.py:25
  26.7 16.4 %collective-permute-start.3 = (f32[16,8192]{1,0:T(8,128)S(1)}, f32[16,8192]{1,0:T(8,128)S(1)}, u32[]{:S(2)}, u32[]{:S(2)}) collective-permute-start(f32[16,8192]{1,0:T(8,128)S(1)} %collective-permute-done.1), channel_id=1, source_target_pairs={{0,120},{8,0},{16,8},{24,16},{32,24},{40,32},{48,40},{56,48},{64,5... | collective-permute-start | bytes 1572872 | tf_op jit(solution)/shard_map/ppermute | solution.py:30
  43.1 15.5 collective-permute-start.4
  43.1 15.5 collective-permute-start.5
  58.6 0.8 copy-start.6
  58.6 14.6 collective-permute-start.6
  59.4 13.8 copy-start.8
  59.4 13.8 collective-permute-start.7
  73.2 0.8 copy-start.10
  73.2 13.7 collective-permute-start.8
  74.0 87.7 %copy-start.12 = (f32[16,8192]{1,0:T(8,128)}, f32[16,8192]{1,0:T(8,128)S(1)}, u32[]{:S(2)}) copy-start(f32[16,8192]{1,0:T(8,128)S(1)} %collective-permute-done.7) | copy-start | bytes 1572868
  74.0 13.6 collective-permute-start.9
  86.9 6.2 copy-start.14
  86.9 12.8 collective-permute-start.10
  87.7 13.6 collective-permute-start.11
  99.7 13.2 collective-permute-start.12
  101.2 115.1 %copy-start.1 = (s32[1024]{0:T(1024)}, s32[1024]{0:T(1024)S(1)}, u32[]{:S(2)}) copy-start(s32[1024]{0:T(1024)S(1)} %broadcast_clamp_fusion.1) | copy-start | bytes 12292
  101.3 435.2 %collective-permute-start.13 = (f32[16,8192]{1,0:T(8,128)}, f32[16,8192]{1,0:T(8,128)}, u32[]{:S(2)}, u32[]{:S(2)}) collective-permute-start(f32[16,8192]{1,0:T(8,128)} %collective-permute-done.11), channel_id=1, source_target_pairs={{0,120},{8,0},{16,8},{24,16},{32,24},{40,32},{48,40},{56,48},{64,5... | collective-permute-start | bytes 1572872 | tf_op jit(solution)/shard_map/ppermute | solution.py:30
  112.9 451.3 %collective-permute-start.14 = (f32[16,8192]{1,0:T(8,128)S(1)}, f32[16,8192]{1,0:T(8,128)}, u32[]{:S(2)}, u32[]{:S(2)}) collective-permute-start(f32[16,8192]{1,0:T(8,128)S(1)} %collective-permute-done.12), channel_id=1, source_target_pairs={{0,8},{8,16},{16,24},{24,32},{32,40},{40,48},{48,56},{56,64},{64,7... | collective-permute-start | bytes 1572872 | tf_op jit(solution)/shard_map/ppermute | solution.py:25
  218.9 77.3 %copy-start.7 = (f32[16,8192]{1,0:T(8,128)S(1)}, f32[16,8192]{1,0:T(8,128)}, u32[]{:S(2)}) copy-start(f32[16,8192]{1,0:T(8,128)} %copy-done.6) | copy-start | bytes 1572868
  245.8 76.4 %copy-start.9 = (f32[16,8192]{1,0:T(8,128)S(1)}, f32[16,8192]{1,0:T(8,128)}, u32[]{:S(2)}) copy-start(f32[16,8192]{1,0:T(8,128)} %copy-done.8) | copy-start | bytes 1572868
  271.9 77.3 %copy-start.11 = (f32[16,8192]{1,0:T(8,128)S(1)}, f32[16,8192]{1,0:T(8,128)}, u32[]{:S(2)}) copy-start(f32[16,8192]{1,0:T(8,128)} %copy-done.10) | copy-start | bytes 1572868
  298.8 76.3 %copy-start.13 = (f32[16,8192]{1,0:T(8,128)S(1)}, f32[16,8192]{1,0:T(8,128)}, u32[]{:S(2)}) copy-start(f32[16,8192]{1,0:T(8,128)} %copy-done.12) | copy-start | bytes 1572868
  324.8 77.2 %copy-start.15 = (f32[16,8192]{1,0:T(8,128)S(1)}, f32[16,8192]{1,0:T(8,128)}, u32[]{:S(2)}) copy-start(f32[16,8192]{1,0:T(8,128)} %copy-done.14) | copy-start | bytes 1572868
  764.7 60.3 %copy-start.17 = (f32[4096]{0:T(1024)S(1)}, f32[4096]{0:T(1024)}, u32[]{:S(2)}) copy-start(f32[4096]{0:T(1024)} %param.15) | copy-start | bytes 49156
  840.4 20.7 %copy-start = (pred[4,256,128]{2,1,0:T(8,128)(4,1)S(1)}, pred[4,256,128]{2,1,0:T(8,128)(4,1)}, u32[]{:S(2)}) copy-start(pred[4,256,128]{2,1,0:T(8,128)(4,1)} %iota_compare_fusion.4) | copy-start | bytes 393220
  840.4 20.7 %copy-start.5 = (f32[128,64]{0,1:T(8,128)S(1)}, f32[128,64]{0,1:T(8,128)}, u32[]{:S(2)}) copy-start(f32[128,64]{0,1:T(8,128)} %custom-call) | copy-start | bytes 98308
  840.4 34.3 %copy-start.20 = (s32[1024]{0:T(1024)S(1)}, s32[1024]{0:T(1024)}, u32[]{:S(2)}) copy-start(s32[1024]{0:T(1024)} %broadcast_clamp_fusion) | copy-start | bytes 12292
  840.4 37.2 %copy-start.18 = (s32[1024]{0:T(1024)S(1)}, s32[1024]{0:T(1024)}, u32[]{:S(2)}) copy-start(s32[1024]{0:T(1024)} %eq.44) | copy-start | bytes 12292
  840.4 178.0 %copy-start.16 = (f32[8192]{0:T(1024)S(1)}, f32[8192]{0:T(1024)}, u32[]{:S(2)}) copy-start(f32[8192]{0:T(1024)} %param.16) | copy-start | bytes 98308
  840.4 178.1 %copy-start.2 = (s32[1024]{0:T(1024)S(1)}, s32[1024]{0:T(1024)}, u32[]{:S(2)}) copy-start(s32[1024]{0:T(1024)} %copy-done.1) | copy-start | bytes 12292
  1107.7 20.7 %copy-start.4 = (f32[128,64]{0,1:T(8,128)S(1)}, f32[128,64]{0,1:T(8,128)}, u32[]{:S(2)}) copy-start(f32[128,64]{0,1:T(8,128)} %custom-call.1) | copy-start | bytes 98308
  1359.0 15.4 copy-start.19
  1374.4 20.7 %copy-start.3 = (f32[128,64]{0,1:T(8,128)S(1)}, f32[128,64]{0,1:T(8,128)}, u32[]{:S(2)}) copy-start(f32[128,64]{0,1:T(8,128)} %custom-call.2) | copy-start | bytes 98308
Sparse Core Ops, SparseCore 0:
  9.7 34.5 all-gather.1
